TPU v7x, 512 devices: a whole 4x4x16 slice. The times are simulated.
512 devices in a mesh: seq: 128 (over z, x, core), tp: 4 (over y).
Axes of the slice: x: 4, y: 4, z: 16, core: 2. Of those that a mesh axis runs over, the one named last changes fastest.
Arguments:
- byte_states: bfloat16 [131072, 1024], P(('seq', 'tp')), may hold values from -24 to 24
- cotangent: bfloat16 [131072, 1024], P(('seq', 'tp')), may hold values from -0.125 to 0.125
- w_up: bfloat16 [1024, 2048], P('seq', 'tp'), may hold values from -0.1875 to 0.1875
- w_down: bfloat16 [2048, 1024], P('tp', 'seq'), may hold values from -0.125 to 0.125
- bounds: int32 [131072], P('seq'), may hold values from 0 to 1, as said below
- owner_counts: int32 [128], replicated, may hold values from 128 to 448, as said below
Outputs:
- hidden: bfloat16 [65536, 2048], P('seq', 'tp')
- grad_up: float32 [1024, 2048], P('seq', 'tp')
- grad_down: float32 [2048, 1024], P('tp', 'seq')
Inputs may be any that keep to these rules, and one draw needn't show every extreme that they name: `bounds`: the first byte of every device's 256 bytes starts a span. The bytes of one device hold at most 96 span starts, and some device holds exactly 96. `owner_counts`: the counts sum to the number of ones in bounds. Owner o's spans are those that start in the bytes of group o (bytes o * 1024 to (o + 1) * 1024 - 1), with at most 32 spans taken from or given to the group before and likewise at the group after; owner 0 begins with span 0; somewhere exactly 32 spans change hands between two neighbouring groups; some owner holds exactly 448 spans.
All inputs are finite; a program needn't handle non-finite values.
Results may differ from a plain program's by a relative error of at most 0.006.
Values may be sent and summed in bfloat16 or wider, within the bound.
A program may use at most 64 MiB of HBM per device.

v0:
```python
import jax
import jax.numpy as jnp
from jax import lax
from jax.sharding import PartitionSpec as P

KLOC = 96
MOVE = 32


epsilon = 1e-05


def passed_along(value, axis, steps):
    count = lax.axis_size(axis)
    initial, last = (max(0, -steps), min(count, count - steps))
    return lax.ppermute(value, axis, [(source, source + steps) for source in range(initial, last)])


def body(byte_states, cotangent, w_up, w_down, bounds, owner_counts):
    local_bytes, feature_count = byte_states.shape
    slice_count = lax.axis_size("tp")
    slice_index = lax.axis_index("tp")
    group_index = lax.axis_index("seq")
    marks = bounds.reshape(slice_count, local_bytes)
    per_slice = jnp.sum(marks, axis=1)
    slice_first = jnp.cumsum(per_slice) - per_slice
    group_total = jnp.sum(per_slice)
    own_marks = lax.dynamic_index_in_dim(marks, slice_index, 0, keepdims=False)
    local_rank = jnp.cumsum(own_marks) - 1
    slot_ids = jnp.arange(KLOC, dtype=jnp.int32)
    in_span = local_rank[None, :] == slot_ids[:, None]
    segment_table = in_span.astype(jnp.bfloat16)
    select_table = (in_span & (own_marks[None, :] == 1)).astype(jnp.bfloat16)
    picked = jnp.dot(select_table, byte_states, preferred_element_type=jnp.float32)
    inverse_rms = lax.rsqrt(jnp.mean(picked * picked, axis=1, keepdims=True) + epsilon)
    normed = (picked * inverse_rms).astype(jnp.bfloat16)
    span_grad = jnp.dot(segment_table, cotangent, preferred_element_type=jnp.float32).astype(
        jnp.bfloat16
    )
    paired = jnp.stack([normed, span_grad])
    gathered = lax.all_gather(paired, "tp", axis=1, tiled=True)
    group_rows = jnp.zeros_like(gathered)
    for position in range(slice_count):
        piece = gathered[:, position * KLOC : (position + 1) * KLOC]
        group_rows = lax.dynamic_update_slice(
            group_rows, piece, (jnp.int32(0), slice_first[position], jnp.int32(0))
        )
    group_capacity = group_rows.shape[1]
    owner_rows = (group_capacity + 2 * MOVE + 127) // 128 * 128
    totals = lax.all_gather(group_total[None], "seq", axis=0, tiled=True)
    earlier_groups = jnp.arange(totals.shape[0], dtype=jnp.int32) < group_index
    before = jnp.sum(jnp.where(earlier_groups, totals, 0))
    owner_ids = jnp.arange(owner_counts.shape[0], dtype=jnp.int32)
    owner_first = jnp.sum(jnp.where(owner_ids < group_index, owner_counts, 0))
    owned_count = jnp.sum(jnp.where(owner_ids == group_index, owner_counts, 0))
    offset = owner_first - before
    aligned = jnp.roll(group_rows, group_capacity - group_total, axis=1)
    from_prev = passed_along(aligned, "seq", 1)[:, group_capacity - MOVE :]
    from_next = passed_along(group_rows, "seq", -1)[:, :MOVE]
    filler = jnp.zeros((2, owner_rows - group_capacity + 2 * MOVE, feature_count), jnp.bfloat16)
    extended = jnp.concatenate([from_prev, group_rows, filler], axis=1)
    placed = lax.dynamic_update_slice(
        jnp.zeros_like(extended), from_next, (jnp.int32(0), MOVE + group_total, jnp.int32(0))
    )
    extended = extended + placed
    owned = lax.dynamic_slice_in_dim(extended, MOVE + offset, owner_rows, 1)
    live_rows = jnp.arange(owner_rows, dtype=jnp.int32) < owned_count
    owned = jnp.where(live_rows[None, :, None], owned, jnp.zeros_like(owned))
    span_rows = owned[0]
    span_cot = owned[1]
    columns = span_rows
    preact = jnp.dot(
        columns, lax.all_gather(w_up, "seq", axis=0, tiled=True), preferred_element_type=jnp.float32
    )
    hidden = jax.nn.silu(preact).astype(jnp.bfloat16)
    columns = span_cot
    back_grad = lax.dot_general(
        columns,
        lax.all_gather(w_down, "seq", axis=1, tiled=True),
        (((1,), (1,)), ((), ())),
        preferred_element_type=jnp.float32,
    )
    gate_sigmoid = jax.nn.sigmoid(preact)
    preact_grad = (back_grad * gate_sigmoid * (1.0 + preact * (1.0 - gate_sigmoid))).astype(
        jnp.bfloat16
    )
    down_terms = lax.dot_general(
        hidden, span_cot, (((0,), (0,)), ((), ())), preferred_element_type=jnp.float32
    )
    grad_down = lax.psum_scatter(down_terms, "seq", scatter_dimension=1, tiled=True)
    columns = span_rows
    grad_up = lax.psum_scatter(
        lax.dot_general(
            columns, preact_grad, (((0,), (0,)), ((), ())), preferred_element_type=jnp.float32
        ),
        "seq",
        scatter_dimension=0,
        tiled=True,
    )
    return (hidden, grad_up, grad_down)


def solution(mesh):
    return jax.shard_map(
        body,
        mesh=mesh,
        in_specs=(
            P(("seq", "tp"), None),
            P(("seq", "tp"), None),
            P("seq", "tp"),
            P("tp", "seq"),
            P("seq"),
            P(),
        ),
        out_specs=(P("seq", "tp"), P("seq", "tp"), P("tp", "seq")),
        check_vma=False,
    )
```

profile of v0, /device:TPU:1, one launch (start us, length us, event | category | flops | bytes accessed | tf_op | source)
XLA Modules:
  0.0 835.2 jit_solution(12977673042637369096)
XLA Ops:
  8.6 1.3 fusion.4
  21.8 29.0 %all-gather.4.cloned.1.call-done = bf16[2,384,1024]{2,1,0:T(8,128)(2,1)} async-done(((bf16[2,96,1024]{2,1,0:T(8,128)(2,1)}), bf16[2,384,1024]{2,1,0:T(8,128)(2,1)}) %all-gather.4.cloned.1.call-update) | async-done | bytes 1572880 | tf_op jit(solution)/shard_map/all_gather | solution.py:41
  50.9 2.3 fusion.22
  53.3 3.4 dynamic_update_slice.15
  56.7 2.4 dynamic_update_slice.16
  59.1 2.4 dynamic_update_slice.17
  61.5 2.3 dynamic_update_slice.18
  63.7 2.8 fusion
  66.5 3.7 collective-permute-start
  70.3 1.9 collective-permute-start.1
  73.5 1.3 dynamic-slice.1
  74.8 1.4 dynamic-update-slice.1
  76.2 31.4 %all-reduce = s32[128]{0:T(128)S(1)} all-reduce(s32[128]{0:T(128)S(1)} %dynamic-update-slice.1), channel_id=1, replica_groups=mesh['seq'=128,'tp'=4] {'seq'}, use_global_device_ids=true, to_apply=%add | all-reduce | flops 128 | bytes 1024
  112.2 1.4 copy-done.1
  113.7 1.0 slice_add_fusion
  114.6 1.8 add.86
  116.4 2.4 dynamic-slice_select_fusion
  118.8 66.4 %all-gather.6.cloned.1.call-done = bf16[1024,512]{1,0:T(8,128)(2,1)} async-done(((bf16[8,512]{1,0:T(8,128)(2,1)}), bf16[1024,512]{1,0:T(8,128)(2,1)}) %all-gather.6.cloned.1.call-update) | async-done | bytes 1048592 | tf_op jit(solution)/shard_map/all_gather | solution.py:73
  185.2 3.0 multiply_convert_fusion
  188.2 126.4 %all-gather.8.cloned.1.call-done = bf16[512,1024]{0,1:T(8,128)(2,1)} async-done(((bf16[512,8]{0,1:T(8,128)(2,1)}), bf16[512,1024]{0,1:T(8,128)(2,1)}) %all-gather.8.cloned.1.call-update) | async-done | bytes 1048592 | tf_op jit(solution)/shard_map/all_gather | solution.py:79
  314.5 4.3 fusion.3
  318.9 2.1 fusion.9
  321.0 244.0 %reduce-scatter.3.cloned.1.call-done = f32[8,512]{1,0:T(8,128)} async-done(((f32[1024,512]{1,0:T(8,128)}), f32[8,512]{1,0:T(8,128)}) %reduce-scatter.3.cloned.1.call-update) | async-done | bytes 16400 | tf_op jit(solution)/shard_map/reduce_scatter | solution.py:92
  565.0 263.6 %reduce-scatter.5.cloned.1.call-done = f32[512,8]{0,1:T(8,128)} async-done(((f32[512,1024]{0,1:T(8,128)}), f32[512,8]{0,1:T(8,128)}) %reduce-scatter.5.cloned.1.call-update) | async-done | bytes 16400 | tf_op jit(solution)/shard_map/reduce_scatter | solution.py:90
  (46 shorter events, 8.7 us)
Async XLA Ops:
  7.2 2.7 copy-start
  7.2 10.8 %copy-start.3 = (s32[1024]{0:T(1024)S(1)}, s32[1024]{0:T(1024)}, u32[]{:S(2)}) copy-start(s32[1024]{0:T(1024)} %param.10) | copy-start | bytes 12292
  7.2 43.7 %all-gather.4.cloned.1.call-start = ((), (), s32[]{:S(2)}) async-start(), calls=%async_computation.2 | async-start | bytes 1966080 | tf_op jit(solution)/shard_map/all_gather | solution.py:41
  11.1 174.0 %all-gather.6.cloned.1.call-start = ((), (), s32[]{:S(2)}) async-start(), calls=%async_computation.3 | async-start | bytes 1056768 | tf_op jit(solution)/shard_map/all_gather | solution.py:73
  11.9 302.6 %all-gather.8.cloned.1.call-start = ((), (), s32[]{:S(2)}) async-start(), calls=%async_computation.4 | async-start | bytes 1056768 | tf_op jit(solution)/shard_map/all_gather | solution.py:79
  61.5 46.7 %copy-start.4 = (s32[128]{0:T(128)S(1)}, s32[128]{0:T(128)}, u32[]{:S(2)}) copy-start(s32[128]{0:T(128)} %param.11) | copy-start | bytes 1540
  66.5 44.3 %collective-permute-start = (bf16[2,384,1024]{2,1,0:T(8,128)(2,1)}, bf16[2,384,1024]{2,1,0:T(8,128)(2,1)}, u32[]{:S(2)}, u32[]{:S(2)}) collective-permute-start(bf16[2,384,1024]{2,1,0:T(8,128)(2,1)} %fusion), channel_id=1, source_target_pairs={{0,4},{4,8},{8,12},{12,16},{16,20},{20,24},{24,28},{28,32},{32,36}... | collective-permute-start | bytes 4718600 | tf_op jit(solution)/shard_map/ppermute | solution.py:16
  70.3 41.9 %collective-permute-start.1 = (bf16[2,384,1024]{2,1,0:T(8,128)(2,1)S(1)}, bf16[2,384,1024]{2,1,0:T(8,128)(2,1)}, u32[]{:S(2)}, u32[]{:S(2)}) collective-permute-start(bf16[2,384,1024]{2,1,0:T(8,128)(2,1)S(1)} %dynamic_update_slice.18), channel_id=1, source_target_pairs={{4,0},{8,4},{12,8},{16,12},{20,16},{24,20},{28,24},{32,28},{36,32}... | collective-permute-start | bytes 4718600 | tf_op jit(solution)/shard_map/ppermute | solution.py:16
  72.2 492.8 %reduce-scatter.3.cloned.1.call-start = ((), (), s32[]{:S(2)}) async-start(), calls=%async_computation.5 | async-start | bytes 2113536 | tf_op jit(solution)/shard_map/reduce_scatter | solution.py:92
  112.2 1.5 copy-start.1
  188.2 130.7 %copy-start.2 = (bf16[512,512]{1,0:T(8,128)(2,1)}, bf16[512,512]{1,0:T(8,128)(2,1)S(1)}, u32[]{:S(2)}) copy-start(bf16[512,512]{1,0:T(8,128)(2,1)S(1)} %get-tuple-element.17) | copy-start | bytes 1572868
  318.8 509.8 %reduce-scatter.5.cloned.1.call-start = ((), (), s32[]{:S(2)}) async-start(), calls=%async_computation.6 | async-start | bytes 2113536 | tf_op jit(solution)/shard_map/reduce_scatter | solution.py:90
Sparse Core Ops, SparseCore 0:
  11.3 39.5 all-gather.3
  53.8 131.2 all-gather.5
  188.2 126.3 all-gather.7
  319.5 245.4 reduce-scatter.2
  570.1 258.5 reduce-scatter.4
where the time goes:
time: 847 us; the launch traced here: 835 us
  waiting for transfers between devices  730 us (86%)
  blocking collectives  31.4 us (4%)
  between operations  24.8 us (3%)
  local copies, waits for them, and re-layouts  21.3 us (3%)
  matrix products  11 us (1%)
  other arithmetic  10.7 us (1%)
    reduce_scatter x1, waiting for transfers between devices, body(): lax.psum_scatter(down_terms, 'seq', scatter_dimension=1, tiled=True)  264 us
    reduce_scatter x1, waiting for transfers between devices, body(): lax.psum_scatter(lax.dot_general(columns, preact_grad, (((0,), (0,)), (()...  244 us
    all_gather x1, waiting for transfers between devices, body(): lax.all_gather(w_down, 'seq', axis=1, tiled=True)  126 us
    all_gather x1, waiting for transfers between devices, body(): lax.all_gather(w_up, 'seq', axis=0, tiled=True)  66.4 us
    unnamed x1, blocking collectives  31.4 us
    all_gather x1, waiting for transfers between devices, body(): gathered = lax.all_gather(paired, 'tp', axis=1, tiled=True)  29 us
  transfers between devices with their start and end apart: 7, of which 5 were waited for; matrix products, arithmetic and copies ran while one was open for 4% of the time, Pallas kernels for 0%

commit v1 on v0

v1 whole, which is shorter than its diff:
```python
import functools

import jax
import jax.numpy as jnp
from jax import lax
from jax.experimental import pallas as pl
from jax.experimental.pallas import tpu as pltpu
from jax.sharding import PartitionSpec as P

MESH = pl.DeviceIdType.MESH
F32 = jnp.float32
BF16 = jnp.bfloat16

KLOC = 96
SLOT = 128
HALF = KLOC // 2
MOVE = 32
NX, NY, NZ = 4, 4, 16
BD = 256
DB = 1024
CW = 256
CAP = 512
NONE = -1.0e6
epsilon = 1e-05


def dot(a, b):
    return jnp.dot(a, b, preferred_element_type=F32)


def dot_nt(a, b):
    return lax.dot_general(a, b, (((1,), (1,)), ((), ())), preferred_element_type=F32)


def iota(shape, dim):
    return lax.broadcasted_iota(jnp.int32, shape, dim)


def kernel(
    bs_hbm, co_hbm, wu_in, wd_in, marks_in, oc_in,
    hid_hbm, gu_out, gd_out,
    bs, co, pw, rw, wu, wd, xn, xc, nt, ct, hh, pg, ff,
    gu32, gub, gd32, gdb,
    ux, ua, ub, u1, u1b, u2, u2b,
    dx, da, db, d1, d1b, d2, d2b,
    hs, hr, ho, hq, fs, fr,
    in_sem, out_sem,
    w_ss, w_rs, ub_ss, ub_rs, ua_ss, ua_rs, ux_ss, ux_rs,
    db_ss, db_rs, da_ss, da_rs, dx_ss, dx_rs,
    y_ss, y_rs, s_ss, s_rs,
    gux_ss, gux_rs, gua_ss, gua_rs, gub_ss, gub_rs,
    gdx_ss, gdx_rs, gda_ss, gda_rs, gdb_ss, gdb_rs,
    h_ss, h_rs, f_ss, f_rs,
):
    s = lax.axis_index("seq")
    t = lax.axis_index("tp")
    c = s % 2
    k = s // 2
    x = k % NX
    z = k // NX
    zm = z % 4
    zh = z // 4
    oc = 1 - c

    def at(zz, xx, cc, tt):
        return (((zz + NZ) % NZ * NX + (xx + NX) % NX) * 2 + cc, (tt + NY) % NY)

    sib = at(z, x, oc, t)
    yp, ym = at(z, x, c, t + 1), at(z, x, c, t - 1)
    xs = [at(z, x + 1, c, t), at(z, x - 1, c, t), at(z, x + 2, c, t)]
    za = [at(z + 1, x, c, t), at(z - 1, x, c, t), at(z + 2, x, c, t), at(z - 2, x, c, t)]
    zb = [at(z + 4, x, c, t), at(z - 4, x, c, t), at(z + 8, x, c, t)]
    nk = NZ * NX
    k_next = ((k + 1) % nk * 2 + c, t)
    k_prev = ((k + nk - 1) % nk * 2 + c, t)

    sends = []

    def send(src, dst, ss, rs, to):
        cp = pltpu.make_async_remote_copy(
            src_ref=src, dst_ref=dst, send_sem=ss, recv_sem=rs, device_id=to, device_id_type=MESH
        )
        cp.start()
        sends.append(cp)
        return cp

    in_bs = pltpu.make_async_copy(bs_hbm, bs, in_sem.at[0])
    in_co = pltpu.make_async_copy(co_hbm, co, in_sem.at[1])
    in_bs.start()
    in_co.start()
    peers = [sib, yp, ym] + xs + za + zb + [k_next, k_prev]
    barrier = pltpu.get_barrier_semaphore()
    for p in peers:
        pl.semaphore_signal(barrier, inc=1, device_id=p, device_id_type=MESH)

    marks = marks_in[...].astype(F32)
    row8 = iota((8, 128), 0)
    lane8 = iota((8, 128), 1)
    own_marks = jnp.concatenate(
        [
            jnp.sum(jnp.where(row8 == 2 * t + h, marks, 0.0), axis=0, keepdims=True)
            for h in range(2)
        ],
        axis=1,
    )
    upto = (iota((BD, BD), 0) <= iota((BD, BD), 1)).astype(F32).astype(BF16)
    rank = dot(jnp.broadcast_to(own_marks, (16, BD)).astype(BF16), upto)[0:1]
    slot_ids = iota((KLOC, BD), 0).astype(F32)
    in_span = jnp.where(slot_ids == rank - 1.0, 1.0, 0.0)
    segment = in_span.astype(BF16)
    select = (in_span * own_marks).astype(BF16)

    per_row = jnp.sum(marks, axis=1, keepdims=True)
    own_counts = jnp.sum(
        jnp.where(row8 // 2 + 4 * c == lane8, per_row, 0.0), axis=0, keepdims=True
    )
    counts16 = jnp.broadcast_to(own_counts, (16, 128)).astype(BF16)
    both_w = jnp.concatenate([wu_in[...].astype(F32), wd_in[...].astype(F32)], axis=0).astype(BF16)
    for h in range(2):
        pw[h, :, 0:CW] = both_w[:, h * CW : (h + 1) * CW]
        pw[h, :, CW : CW + 128] = counts16

    in_bs.wait()
    picked = dot(select, bs[...])
    inverse_rms = lax.rsqrt(jnp.mean(picked * picked, axis=1, keepdims=True) + epsilon)
    xn[c, t] = (picked * inverse_rms).astype(BF16)

    pl.semaphore_wait(barrier, len(peers))

    w_cp = send(pw.at[oc], rw, w_ss, w_rs, sib)

    def send_own(buf, kind):
        own = buf.at[c, t]
        return (
            send(own, own, y_ss.at[kind, 0], y_rs.at[kind, 0], yp),
            send(own, own, y_ss.at[kind, 1], y_rs.at[kind, 1], ym),
            send(own, own, s_ss.at[kind, 0], s_rs.at[kind, 0], sib),
        )

    own_n = send_own(xn, 0)
    in_co.wait()
    xc[c, t] = dot(segment, co[...]).astype(BF16)
    own_c = send_own(xc, 1)

    tp_, tm_, t2_ = (t + 1) % NY, (t + NY - 1) % NY, (t + 2) % NY

    def forward(buf, kind, own):
        own[0].wait_recv()
        a = buf.at[c, tm_, 0:HALF]
        f0 = send(a, a, y_ss.at[kind, 2], y_rs.at[kind, 2], yp)
        a = buf.at[c, tm_]
        g0 = send(a, a, s_ss.at[kind, 1], s_rs.at[kind, 1], sib)
        own[1].wait_recv()
        a = buf.at[c, tp_, HALF:KLOC]
        f1 = send(a, a, y_ss.at[kind, 3], y_rs.at[kind, 3], ym)
        a = buf.at[c, tp_]
        g1 = send(a, a, s_ss.at[kind, 2], s_rs.at[kind, 2], sib)
        return f0, f1, g0, g1

    def forward_far(buf, kind, f):
        f[0].wait_recv()
        a = buf.at[c, t2_, 0:HALF]
        g2 = send(a, a, s_ss.at[kind, 3], s_rs.at[kind, 3], sib)
        f[1].wait_recv()
        a = buf.at[c, t2_, HALF:KLOC]
        g3 = send(a, a, s_ss.at[kind, 4], s_rs.at[kind, 4], sib)
        return g2, g3

    eye = (iota((256, 256), 0) == iota((256, 256), 1)).astype(F32).astype(BF16)
    filler = jnp.zeros((SLOT - KLOC, DB), BF16)

    def rows_of(buf, cc, tt):
        return jnp.concatenate([buf[cc, tt], filler], axis=0)

    def transpose(buf, out, cc, tt):
        rows = rows_of(buf, cc, tt)
        for j in range(DB // 256):
            out[cc * 4 + tt, j * 256 : (j + 1) * 256, :] = dot_nt(
                eye, rows[:, j * 256 : (j + 1) * 256]
            ).astype(BF16)

    def up(cc, tt):
        v = dot(rows_of(xn, cc, tt), wu[...].reshape(DB, CW))
        sg = jax.nn.sigmoid(v)
        hh[cc * 4 + tt] = (v * sg).astype(BF16)
        ff[cc * 4 + tt] = sg * (1.0 + v * (1.0 - sg))

    def back(cc, tt):
        v = dot(rows_of(xc, cc, tt), wd[:, :, :, :, 0:CW].reshape(DB, CW))
        pg[cc * 4 + tt] = (v * ff[cc * 4 + tt]).astype(BF16)

    w_cp.wait_recv()
    mine, other = pw[c].astype(F32), rw[...].astype(F32)
    low, high = jnp.where(c == 0, mine, other), jnp.where(c == 0, other, mine)
    wu[zh, zm, x] = jnp.concatenate([low[0:8, 0:CW], high[0:8, 0:CW]], axis=0).astype(BF16)
    counts_f = low[0:8, CW:] + high[0:8, CW:]
    wd[zh, zm, x, :, 0:CW] = jnp.concatenate([low[8:16, 0:CW], high[8:16, 0:CW]], axis=0).astype(BF16)
    wd[zh, zm, x, :, CW:] = jnp.concatenate([counts_f, counts_f], axis=0).astype(BF16)

    def gather_zb(buf, ss, rs):
        a = buf.at[zh, zm, x]
        return [send(a, a, ss.at[j], rs.at[j], zb[j]) for j in range(3)]

    def gather_za(parts, ss, rs):
        full, first, second = parts
        return [
            send(full, full, ss.at[0], rs.at[0], za[0]),
            send(full, full, ss.at[1], rs.at[1], za[1]),
            send(first, first, ss.at[2], rs.at[2], za[2]),
            send(second, second, ss.at[3], rs.at[3], za[3]),
        ]

    def gather_x(a, ss, rs):
        return [send(a, a, ss.at[j], rs.at[j], xs[j]) for j in range(3)]

    def arrive(cps):
        for cp in cps:
            cp.wait_recv()

    w_u = gather_zb(wu, ub_ss, ub_rs)
    w_d = gather_zb(wd, db_ss, db_rs)
    transpose(xn, nt, c, t)
    transpose(xc, ct, c, t)
    arrive(w_u)
    w_u = gather_za(
        (wu.at[:, zm, x], wu.at[0:2, zm, x], wu.at[2:4, zm, x]), ua_ss, ua_rs
    )
    arrive(w_d)
    w_d = gather_x(wd.at[:, zm, x], dx_ss, dx_rs)

    far_n = forward(xn, 0, own_n)
    arrive(w_u)
    w_u = gather_x(wu.at[:, :, x], ux_ss, ux_rs)
    arrive(w_d)
    w_d = gather_za((wd.at[:, zm], wd.at[0:2, zm], wd.at[2:4, zm]), da_ss, da_rs)
    own_n[2].wait_recv()
    transpose(xn, nt, oc, t)
    transpose(xn, nt, c, tm_)
    transpose(xn, nt, c, tp_)

    far_c = forward(xc, 1, own_c)
    own_c[2].wait_recv()
    transpose(xc, ct, oc, t)
    transpose(xc, ct, c, tm_)
    transpose(xc, ct, c, tp_)
    far_n[2].wait_recv()
    far_n[3].wait_recv()
    transpose(xn, nt, oc, tm_)
    transpose(xn, nt, oc, tp_)

    arrive(w_u)
    last_n = forward_far(xn, 0, far_n)
    for cc, tt in ((c, t), (oc, t), (c, tm_), (c, tp_), (oc, tm_), (oc, tp_), (c, t2_)):
        up(cc, tt)
    transpose(xn, nt, c, t2_)
    arrive(w_d)
    last_c = forward_far(xc, 1, far_c)
    far_c[2].wait_recv()
    far_c[3].wait_recv()
    transpose(xc, ct, oc, tm_)
    transpose(xc, ct, oc, tp_)
    transpose(xc, ct, c, t2_)
    for cc, tt in ((c, t), (oc, t), (c, tm_), (c, tp_), (oc, tm_), (oc, tp_), (c, t2_)):
        back(cc, tt)
    last_n[0].wait_recv()
    last_n[1].wait_recv()
    up(oc, t2_)
    transpose(xn, nt, oc, t2_)
    last_c[0].wait_recv()
    last_c[1].wait_recv()
    transpose(xc, ct, oc, t2_)

    def grad(tt_ref, right_ref, g32, gb):
        right = right_ref[...].reshape(8 * SLOT, CW)
        for i in range(4):
            left = jnp.concatenate(
                [tt_ref[b, i * 256 : (i + 1) * 256, :] for b in range(8)], axis=1
            )
            r = dot(left, right).reshape(4, NX, 16, CW)
            g32[i] = r
            gb[i] = r.astype(BF16)

    c1, c2, c3 = (zm + 1) % 4, (zm + 2) % 4, (zm + 3) % 4
    x1, x2, x3 = (x + 1) % 4, (x + 2) % 4, (x + 3) % 4
    h1, h2, h3 = (zh + 1) % 4, (zh + 2) % 4, (zh + 3) % 4

    def scatter_za(buf, rest, into, ss, rs):
        def part(zs, m):
            return buf.at[zs, m] if rest is None else buf.at[zs, m, rest]

        allz, lo, hi = slice(0, 4), slice(0, 2), slice(2, 4)
        return [
            send(part(allz, c1), into.at[0], ss.at[0], rs.at[0], za[0]),
            send(part(allz, c3), into.at[1], ss.at[1], rs.at[1], za[1]),
            send(part(lo, c2), into.at[2, 0:2], ss.at[2], rs.at[2], za[2]),
            send(part(hi, c2), into.at[2, 2:4], ss.at[3], rs.at[3], za[3]),
        ]

    def scatter_zb(buf, into, ss, rs):
        return [
            send(buf.at[h1], into.at[0], ss.at[0], rs.at[0], zb[0]),
            send(buf.at[h3], into.at[1], ss.at[1], rs.at[1], zb[1]),
            send(buf.at[h2], into.at[2], ss.at[2], rs.at[2], zb[2]),
        ]

    def total(own, into):
        return own + into[0].astype(F32) + into[1].astype(F32) + into[2].astype(F32)

    grad(ct, hh, gd32, gdb)
    g_d = scatter_za(gdb, None, da, gda_ss, gda_rs)
    back(oc, t2_)
    grad(nt, pg, gu32, gub)
    g_u = [
        send(gub.at[:, :, xx], ux.at[j], gux_ss.at[j], gux_rs.at[j], xs[j])
        for j, xx in enumerate((x1, x3, x2))
    ]

    chips = wd[:, :, :, :, CW:].reshape(NZ * NX * 16, 128).astype(F32)
    chip_row = iota((NZ * NX * 16, 128), 0)
    chip_lane = iota((NZ * NX * 16, 128), 1)
    first_rows = chip_row % 16 == 0
    ahead = jnp.where(first_rows & (chip_row // 16 < k) & (chip_lane < 8), chips, 0.0)
    before_a = jnp.sum(jnp.sum(ahead, axis=0, keepdims=True), axis=1, keepdims=True)
    here = jnp.sum(
        jnp.where(first_rows & (chip_row // 16 == k), chips, 0.0), axis=0, keepdims=True
    )
    lane1 = iota((1, 128), 1)
    slot1 = lane1.astype(F32)
    pos, totals = [], []
    for g in range(2):
        first = jnp.zeros((1, 1), F32)
        parts = []
        for p in range(4):
            n = jnp.sum(jnp.where(lane1 == 4 * g + p, here, 0.0), axis=1, keepdims=True)
            parts.append(jnp.where(slot1 < n, slot1 + first, NONE))
            first = first + n
        pos.append(jnp.concatenate(parts, axis=1))
        totals.append(first)
    owners = oc_in[...].astype(F32)
    owner_first = jnp.sum(jnp.where(lane1 < 2 * k, owners, 0.0), axis=1, keepdims=True)
    owned = [
        jnp.sum(jnp.where(lane1 == 2 * k + g, owners, 0.0), axis=1, keepdims=True)
        for g in range(2)
    ]
    shift = [owner_first - before_a, owner_first + owned[0] - before_a - totals[0]]
    end_ids = iota((MOVE, CAP), 0).astype(F32)
    group_rows = [hh[4 * g : 4 * g + 4].reshape(CAP, CW) for g in range(2)]

    def ends(g, base):
        table = jnp.where(end_ids + base == pos[g], 1.0, 0.0).astype(BF16)
        return dot(table, group_rows[g]).astype(BF16)

    hs[0] = ends(0, 0.0)
    hs[1] = ends(1, totals[1] - MOVE)
    h_p = send(hs.at[0], hr.at[0], h_ss.at[0], h_rs.at[0], k_prev)
    h_n = send(hs.at[1], hr.at[1], h_ss.at[1], h_rs.at[1], k_next)
    first_b = ends(1, 0.0)
    last_a = ends(0, totals[0] - MOVE)

    row_ids = iota((CAP, CAP), 0).astype(F32)
    end_row = iota((CAP, 2 * MOVE), 0).astype(F32)
    end_lane1 = iota((1, 2 * MOVE), 1)
    end_at = end_lane1.astype(F32)

    def place(g, edge):
        inner = jnp.where(
            (row_ids + shift[g] == pos[g]) & (row_ids < owned[g]), 1.0, 0.0
        ).astype(BF16)
        end_pos = jnp.where(end_lane1 < MOVE, end_at - MOVE, end_at - MOVE + totals[g])
        outer = jnp.where(
            (end_row + shift[g] == end_pos) & (end_row < owned[g]), 1.0, 0.0
        ).astype(BF16)
        ho[g] = (dot(inner, group_rows[g]) + dot(outer, edge)).astype(BF16)

    h_p.wait_recv()
    h_n.wait_recv()
    place(0, jnp.concatenate([hr[1], first_b], axis=0))
    place(1, jnp.concatenate([last_a, hr[0]], axis=0))
    h_s = send(ho.at[oc], hq, h_ss.at[2], h_rs.at[2], sib)
    out_own = pltpu.make_async_copy(
        ho.at[c], hid_hbm.at[:, pl.ds(pl.multiple_of(c * CW, CW), CW)], out_sem.at[0]
    )
    out_own.start()

    arrive(g_d)
    r = total(gd32[:, zm], da)
    d1[...] = r
    d1b[...] = r.astype(BF16)
    g_d = [
        send(d1b.at[:, xx], dx.at[j], gdx_ss.at[j], gdx_rs.at[j], xs[j])
        for j, xx in enumerate((x1, x3, x2))
    ]
    arrive(g_u)
    r = total(gu32[:, :, x], ux)
    u1[...] = r
    u1b[...] = r.astype(BF16)
    g_u = scatter_za(u1b, None, ua, gua_ss, gua_rs)

    arrive(g_d)
    r = total(d1[:, x], dx)
    d2[...] = r
    d2b[...] = r.astype(BF16)
    g_d = scatter_zb(d2b, db, gdb_ss, gdb_rs)
    arrive(g_u)
    r = total(u1[:, zm], ua)
    u2[...] = r
    u2b[...] = r.astype(BF16)
    g_u = scatter_zb(u2b, ub, gub_ss, gub_rs)

    h_s.wait_recv()
    out_sib = pltpu.make_async_copy(
        hq, hid_hbm.at[:, pl.ds(pl.multiple_of(oc * CW, CW), CW)], out_sem.at[1]
    )
    out_sib.start()

    arrive(g_d)
    r = total(d2[zh], db)
    fs[1, 0] = r[0:8]
    fs[1, 1] = r[8:16]
    arrive(g_u)
    r = total(u2[zh], ub)
    fs[0, 0] = r[0:8]
    fs[0, 1] = r[8:16]
    f_cp = send(fs.at[:, oc], fr, f_ss, f_rs, sib)
    f_cp.wait_recv()
    for i, out in enumerate((gu_out, gd_out)):
        mine, other = fs[i, c], fr[i]
        out[:, 0:CW] = jnp.where(c == 0, mine, other)
        out[:, CW:] = jnp.where(c == 0, other, mine)

    for cp in sends:
        cp.wait_send()
    out_own.wait()
    out_sib.wait()


def body(byte_states, cotangent, w_up, w_down, bounds, owner_counts):
    vmem = pl.BlockSpec(memory_space=pltpu.VMEM)
    hbm = pl.BlockSpec(memory_space=pl.ANY)
    dma = pltpu.SemaphoreType.DMA
    scratch = [
        pltpu.VMEM((BD, DB), BF16),
        pltpu.VMEM((BD, DB), BF16),
        pltpu.VMEM((2, 16, CW + 128), BF16),
        pltpu.VMEM((16, CW + 128), BF16),
        pltpu.VMEM((4, 4, NX, 16, CW), BF16),
        pltpu.VMEM((4, 4, NX, 16, CW + 128), BF16),
        pltpu.VMEM((2, NY, KLOC, DB), BF16),
        pltpu.VMEM((2, NY, KLOC, DB), BF16),
        pltpu.VMEM((8, DB, SLOT), BF16),
        pltpu.VMEM((8, DB, SLOT), BF16),
        pltpu.VMEM((8, SLOT, CW), BF16),
        pltpu.VMEM((8, SLOT, CW), BF16),
        pltpu.VMEM((8, SLOT, CW), F32),
        pltpu.VMEM((4, 4, NX, 16, CW), F32),
        pltpu.VMEM((4, 4, NX, 16, CW), BF16),
        pltpu.VMEM((4, 4, NX, 16, CW), F32),
        pltpu.VMEM((4, 4, NX, 16, CW), BF16),
        pltpu.VMEM((3, 4, 4, 16, CW), BF16),
        pltpu.VMEM((3, 4, 16, CW), BF16),
        pltpu.VMEM((3, 16, CW), BF16),
        pltpu.VMEM((4, 4, 16, CW), F32),
        pltpu.VMEM((4, 4, 16, CW), BF16),
        pltpu.VMEM((4, 16, CW), F32),
        pltpu.VMEM((4, 16, CW), BF16),
        pltpu.VMEM((3, 4, 16, CW), BF16),
        pltpu.VMEM((3, 4, NX, 16, CW), BF16),
        pltpu.VMEM((3, 16, CW), BF16),
        pltpu.VMEM((4, NX, 16, CW), F32),
        pltpu.VMEM((4, NX, 16, CW), BF16),
        pltpu.VMEM((4, 16, CW), F32),
        pltpu.VMEM((4, 16, CW), BF16),
        pltpu.VMEM((2, MOVE, CW), BF16),
        pltpu.VMEM((2, MOVE, CW), BF16),
        pltpu.VMEM((2, CAP, CW), BF16),
        pltpu.VMEM((CAP, CW), BF16),
        pltpu.VMEM((2, 2, 8, CW), F32),
        pltpu.VMEM((2, 8, CW), F32),
        dma((2,)),
        dma((2,)),
        dma, dma,
        dma((3,)), dma((3,)), dma((4,)), dma((4,)), dma((3,)), dma((3,)),
        dma((3,)), dma((3,)), dma((4,)), dma((4,)), dma((3,)), dma((3,)),
        dma((2, 4)), dma((2, 4)), dma((2, 5)), dma((2, 5)),
        dma((3,)), dma((3,)), dma((4,)), dma((4,)), dma((3,)), dma((3,)),
        dma((3,)), dma((3,)), dma((4,)), dma((4,)), dma((3,)), dma((3,)),
        dma((3,)), dma((3,)), dma, dma,
    ]
    hidden, grad_up, grad_down = pl.pallas_call(
        kernel,
        out_shape=(
            jax.ShapeDtypeStruct((CAP, 2 * CW), BF16),
            jax.ShapeDtypeStruct((8, 2 * CW), F32),
            jax.ShapeDtypeStruct((8, 2 * CW), F32),
        ),
        in_specs=[hbm, hbm, vmem, vmem, vmem, vmem],
        out_specs=(hbm, vmem, vmem),
        scratch_shapes=scratch,
        compiler_params=pltpu.CompilerParams(
            collective_id=0, has_side_effects=True, vmem_limit_bytes=48 * 1024 * 1024
        ),
        cost_estimate=pl.CostEstimate(
            flops=4 * 10**9, bytes_accessed=2 * 1024 * 1024, transcendentals=262144
        ),
    )(
        byte_states,
        cotangent,
        w_up,
        w_down.T,
        bounds.reshape(8, 128),
        owner_counts.reshape(1, 128),
    )
    return hidden, grad_up, grad_down.T


def solution(mesh):
    return jax.shard_map(
        body,
        mesh=mesh,
        in_specs=(
            P(("seq", "tp"), None),
            P(("seq", "tp"), None),
            P("seq", "tp"),
            P("tp", "seq"),
            P("seq"),
            P(),
        ),
        out_specs=(P("seq", "tp"), P("seq", "tp"), P("tp", "seq")),
        check_vma=False,
    )
```

time: 847 us -> 75.2 us (0.09); the launches traced: 835 us -> 74.8 us
  waiting for transfers between devices: 730 us -> 0 us
  Pallas kernels: 0 us -> 68 us
  blocking collectives: 31.4 us -> 0 us
  between operations: 24.8 us -> 0.66 us
  local copies, waits for them, and re-layouts: 21.3 us -> 6.15 us
  matrix products: 11 us -> 0 us
  other arithmetic: 10.7 us -> 0 us
    reduce_scatter x2 -> x0, waiting for transfers between devices: 508 us -> none  [the longest x1 264 us: body(): lax.psum_scatter(down_terms, 'seq', scatter_dimension=1, tiled=True)]
    all_gather x3 -> x0, waiting for transfers between devices: 222 us -> none  [the longest x1 126 us: body(): lax.all_gather(w_down, 'seq', axis=1, tiled=True)]
    pallas_call x0 -> x1, Pallas kernels: none -> 68 us  [body(): pl.pallas_call(kernel, out_shape=(jax.ShapeDtypeStruct((CAP, 2 * CW), BF1...]
    unnamed x1 -> x0, blocking collectives: 31.4 us -> none
    dot_general x5 -> x0, matrix products: 11 us -> none  [the longest x1 4.28 us: body(): lax.dot_general(columns, preact_grad, (((0,), (0,)), ((), ())), preferred...]
    dynamic_update_slice x4 -> x0, local copies, waits for them, and re-layouts: 10.4 us -> none  [body(): lax.dynamic_update_slice(group_rows, piece, (jnp.int32(0), slice_first[po...]
  transfers between devices with their start and end apart: 7 -> 0, of which waited for: 5 -> 0; matrix products, arithmetic and copies ran while one was open for 4% -> 0% of each run, Pallas kernels for 0% -> 0%
where the time goes in v1:
time: 75.2 us; the launch traced here: 74.8 us
  Pallas kernels  68 us (90%)
  local copies, waits for them, and re-layouts  6.15 us (8%)
    pallas_call x1, Pallas kernels, body(): pl.pallas_call(kernel, out_shape=(jax.ShapeDtypeStruct((CAP, 2 * CW), BF1...  68 us
    unnamed x15, local copies, waits for them, and re-layouts  6.15 us

profile of v1, /device:TPU:1, one launch (start us, length us, event | category | flops | bytes accessed | tf_op | source)
XLA Modules:
  0.0 74.8 jit_solution(11213130492927348354)
XLA Ops:
  0.6 0.0 copy-start.4
  0.6 0.0 copy-start.5
  0.7 0.7 copy-done.4
  1.3 0.0 copy-done.5
  1.3 0.0 copy-start
  1.3 1.0 %copy-done = bf16[256,1024]{1,0:T(8,128)(2,1)S(1)} copy-done((bf16[256,1024]{1,0:T(8,128)(2,1)S(1)}, bf16[256,1024]{1,0:T(8,128)(2,1)}, u32[]{:S(2)}) %copy-start) | copy-done | bytes 524312
  2.4 0.0 copy-start.1
  2.4 1.0 %copy-done.1 = bf16[256,1024]{1,0:T(8,128)(2,1)S(1)} copy-done((bf16[256,1024]{1,0:T(8,128)(2,1)S(1)}, bf16[256,1024]{1,0:T(8,128)(2,1)}, u32[]{:S(2)}) %copy-start.1) | copy-done | bytes 524312
  3.4 0.0 copy-start.2
  3.4 0.7 copy-done.2
  4.1 0.0 copy-start.3
  4.1 0.7 copy-done.3
  4.8 68.0 %shard_map.85 = (bf16[512,512]{1,0:T(8,128)(2,1)S(1)}, f32[8,512]{1,0:T(8,128)S(1)}, f32[8,512]{1,0:T(8,128)S(1)}) custom-call(bf16[256,1024]{1,0:T(8,128)(2,1)S(1)} %copy-done, bf16[256,1024]{1,0:T(8,128)(2,1)S(1)} %copy-done.1, bf16[8,512]{1,0:T(8,128)(2,1)S(1)} %copy-done.2, bf16[8,512]{1,0:T(8,128)(2,1)S(1)} %bitcast.5, s32[8,128]{1,0:T(8,128)S(1)} %bitcast.6, ...), custom_call_target="tpu_custom_call" | custom-call | flops 4000000000 | bytes 2097152 | tf_op jit(solution)/shard_map/pallas_call | solution.py:489
  72.8 0.8 %copy.12 = bf16[512,512]{1,0:T(8,128)(2,1)} copy(bf16[512,512]{1,0:T(8,128)(2,1)S(1)} %get-tuple-element.12) | data formatting | bytes 1048576
  73.6 0.6 copy.13
  74.2 0.6 copy.14
Async XLA Ops:
  0.6 0.7 copy-start.4
  0.6 0.7 copy-start.5
  1.3 1.0 %copy-start = (bf16[256,1024]{1,0:T(8,128)(2,1)S(1)}, bf16[256,1024]{1,0:T(8,128)(2,1)}, u32[]{:S(2)}) copy-start(bf16[256,1024]{1,0:T(8,128)(2,1)} %bs_hbm.1) | copy-start | bytes 1572868
  2.4 1.0 %copy-start.1 = (bf16[256,1024]{1,0:T(8,128)(2,1)S(1)}, bf16[256,1024]{1,0:T(8,128)(2,1)}, u32[]{:S(2)}) copy-start(bf16[256,1024]{1,0:T(8,128)(2,1)} %co_hbm.1) | copy-start | bytes 1572868
  3.4 0.7 copy-start.2
  4.1 0.7 copy-start.3

commit v2 on v1

v2 whole, which is shorter than its diff:
```python
import functools

import jax
import jax.numpy as jnp
from jax import lax
from jax.experimental import pallas as pl
from jax.experimental.pallas import tpu as pltpu
from jax.sharding import PartitionSpec as P

MESH = pl.DeviceIdType.MESH
F32 = jnp.float32
BF16 = jnp.bfloat16

KLOC = 96
SLOT = 128
HALF = KLOC // 2
MOVE = 32
NX, NY, NZ = 4, 4, 16
BD = 256
DB = 1024
CW = 256
CAP = 512
NONE = -1.0e6
epsilon = 1e-05


def dot(a, b):
    return jnp.dot(a, b, preferred_element_type=F32)


def dot_nt(a, b):
    return lax.dot_general(a, b, (((1,), (1,)), ((), ())), preferred_element_type=F32)


def iota(shape, dim):
    return lax.broadcasted_iota(jnp.int32, shape, dim)


ORDER = (2, 1, 3, 0)


def kernel(
    bs_hbm, co_hbm, wu_in, wd_in, marks_hbm, oc_hbm,
    hid_hbm, gu_out, gd_out,
    bs, co, marks_in, oc_in, pw, rw, wur, wdr, wu, wd, xn, xc, nt, ct, hh, pg, ff,
    gu32, gub, gd32, gdb,
    ux, ua, ua2, ub, u1, u1b, u2b,
    dx, da, da2, db, d1, d1b, d2b,
    hs, hr, ho, hq, cx, cz, sb, rb, s0, r0,
    in_sem, out_sem,
    w_ss, w_rs,
    wuz_ss, wuz_rs, wua_ss, wua_rs, wux_ss, wux_rs,
    wdz_ss, wdz_rs, wda_ss, wda_rs, wdx_ss, wdx_rs,
    y_ss, y_rs, s_ss, s_rs,
    gux_ss, gux_rs, gua_ss, gua_rs, gub_ss, gub_rs,
    gdx_ss, gdx_rs, gda_ss, gda_rs, gdb_ss, gdb_rs,
    h_ss, h_rs, f_ss, f_rs, c_ss, c_rs,
):
    s = lax.axis_index("seq")
    t = lax.axis_index("tp")
    c = s % 2
    k = s // 2
    x = k % NX
    z = k // NX
    oc = 1 - c

    def at(zz, xx, cc, tt):
        return (((zz + NZ) % NZ * NX + (xx + NX) % NX) * 2 + cc, (tt + NY) % NY)

    sib = at(z, x, oc, t)
    yp, ym = at(z, x, c, t + 1), at(z, x, c, t - 1)
    xs = [at(z, x + 1, c, t), at(z, x - 1, c, t), at(z, x + 2, c, t)]
    z1p, z1m, z2p, z2m = (at(z + d, x, c, t) for d in (1, -1, 2, -2))
    z4p, z4m, z4p_other, z4m_other = (at(z + d, x, cc, t) for cc in (c, oc) for d in (4, -4))
    x_of = [(x + 1) % NX, (x + 3) % NX, (x + 2) % NX]
    nk = NZ * NX
    k_next = ((k + 1) % nk * 2 + c, t)
    k_prev = ((k + nk - 1) % nk * 2 + c, t)

    sends = []

    def send(src, dst, ss, rs, to):
        cp = pltpu.make_async_remote_copy(
            src_ref=src, dst_ref=dst, send_sem=ss, recv_sem=rs, device_id=to, device_id_type=MESH
        )
        cp.start()
        sends.append(cp)
        return cp

    peers = [sib, yp, ym] + xs + [z1p, z1m, z2p, z2m]
    peers += [z4p, z4m, z4p_other, z4m_other, k_next, k_prev]
    barrier = pltpu.get_barrier_semaphore()
    for p in peers:
        pl.semaphore_signal(barrier, inc=1, device_id=p, device_id_type=MESH)
    in_cps = [
        pltpu.make_async_copy(a, b, in_sem.at[i])
        for i, (a, b) in enumerate(
            ((marks_hbm, marks_in), (oc_hbm, oc_in), (bs_hbm, bs), (co_hbm, co))
        )
    ]
    for cp in in_cps:
        cp.start()
    in_cps[0].wait()

    marks = marks_in[...].astype(F32)
    row8 = iota((8, 128), 0)
    lane8 = iota((8, 128), 1)
    per_row = jnp.sum(marks, axis=1, keepdims=True)
    own_counts = jnp.sum(
        jnp.where(row8 // 2 + 4 * c == lane8, per_row, 0.0), axis=0, keepdims=True
    )
    counts16 = jnp.broadcast_to(own_counts, (16, 128)).astype(BF16)
    both_w = jnp.concatenate([wu_in[...].astype(F32), wd_in[...].astype(F32)], axis=0).astype(BF16)
    for h in range(2):
        pw[h, :, 0:CW] = both_w[:, h * CW : (h + 1) * CW]
        pw[h, :, CW : CW + 128] = counts16

    pl.semaphore_wait(barrier, len(peers))
    w_cp = send(pw.at[oc], rw, w_ss, w_rs, sib)

    own_marks = jnp.concatenate(
        [
            jnp.sum(jnp.where(row8 == 2 * t + h, marks, 0.0), axis=0, keepdims=True)
            for h in range(2)
        ],
        axis=1,
    )
    upto = (iota((BD, BD), 0) <= iota((BD, BD), 1)).astype(F32).astype(BF16)
    rank = dot(jnp.broadcast_to(own_marks, (16, BD)).astype(BF16), upto)[0:1]
    slot_ids = iota((KLOC, BD), 0).astype(F32)
    in_span = jnp.where(slot_ids == rank - 1.0, 1.0, 0.0)
    segment = in_span.astype(BF16)
    select = (in_span * own_marks).astype(BF16)

    in_cps[2].wait()
    picked = dot(select, bs[...])
    inverse_rms = lax.rsqrt(jnp.mean(picked * picked, axis=1, keepdims=True) + epsilon)
    xn[c, t] = (picked * inverse_rms).astype(BF16)

    def send_own(buf, kind):
        own = buf.at[c, t]
        return (
            send(own, own, y_ss.at[kind, 0], y_rs.at[kind, 0], yp),
            send(own, own, y_ss.at[kind, 1], y_rs.at[kind, 1], ym),
            send(own, own, s_ss.at[kind, 0], s_rs.at[kind, 0], sib),
        )

    own_n = send_own(xn, 0)
    in_cps[3].wait()
    xc[c, t] = dot(segment, co[...]).astype(BF16)
    own_c = send_own(xc, 1)

    tp_, tm_, t2_ = (t + 1) % NY, (t + NY - 1) % NY, (t + 2) % NY

    def forward(buf, kind, own):
        own[0].wait_recv()
        a = buf.at[c, tm_, 0:HALF]
        f0 = send(a, a, y_ss.at[kind, 2], y_rs.at[kind, 2], yp)
        a = buf.at[c, tm_]
        g0 = send(a, a, s_ss.at[kind, 1], s_rs.at[kind, 1], sib)
        own[1].wait_recv()
        a = buf.at[c, tp_, HALF:KLOC]
        f1 = send(a, a, y_ss.at[kind, 3], y_rs.at[kind, 3], ym)
        a = buf.at[c, tp_]
        g1 = send(a, a, s_ss.at[kind, 2], s_rs.at[kind, 2], sib)
        return f0, f1, g0, g1

    def forward_far(buf, kind, f):
        f[0].wait_recv()
        a = buf.at[c, t2_, 0:HALF]
        g2 = send(a, a, s_ss.at[kind, 3], s_rs.at[kind, 3], sib)
        f[1].wait_recv()
        a = buf.at[c, t2_, HALF:KLOC]
        g3 = send(a, a, s_ss.at[kind, 4], s_rs.at[kind, 4], sib)
        return g2, g3

    eye = (iota((256, 256), 0) == iota((256, 256), 1)).astype(F32).astype(BF16)
    filler = jnp.zeros((SLOT - KLOC, DB), BF16)

    def rows_of(buf, cc, tt):
        return jnp.concatenate([buf[cc, tt], filler], axis=0)

    def transpose(buf, out, cc, tt):
        rows = rows_of(buf, cc, tt)
        for j in range(DB // 256):
            out[cc * 4 + tt, j * 256 : (j + 1) * 256, :] = dot_nt(
                eye, rows[:, j * 256 : (j + 1) * 256]
            ).astype(BF16)

    def up(cc, tt):
        v = dot(rows_of(xn, cc, tt), wu[...])
        sg = jax.nn.sigmoid(v)
        hh[cc * 4 + tt] = (v * sg).astype(BF16)
        ff[cc * 4 + tt] = sg * (1.0 + v * (1.0 - sg))

    def back(cc, tt):
        v = dot(rows_of(xc, cc, tt), wd[...])
        pg[cc * 4 + tt] = (v * ff[cc * 4 + tt]).astype(BF16)

    def arrive(cps):
        for cp in cps:
            cp.wait_recv()

    w_cp.wait_recv()
    mine, other = pw[c].astype(F32), rw[...].astype(F32)
    low, high = jnp.where(c == 0, mine, other), jnp.where(c == 0, other, mine)
    wur[0, 1, x] = jnp.concatenate([low[0:8, 0:CW], high[0:8, 0:CW]], axis=0).astype(BF16)
    wdr[0, 1, x] = jnp.concatenate([low[8:16, 0:CW], high[8:16, 0:CW]], axis=0).astype(BF16)
    cx[x] = low[0:1, CW:] + high[0:1, CW:]

    def stride(src, dst, j, to):
        return [
            send(b.at[src, 1, x], b.at[dst, 1, x], ss.at[j], rs.at[j], to)
            for b, ss, rs in ((wur, wuz_ss, wuz_rs), (wdr, wdz_ss, wdz_rs))
        ]

    w_z = {3: stride(0, 3, 0, z4p), 1: stride(0, 1, 1, z4m)}
    c_x = [send(cx.at[x], cx.at[x], c_ss.at[j], c_rs.at[j], xs[j]) for j in range(3)]

    def spread_near(part, m, ss, rs):
        cps = {
            (m, 0): send(part(m, 1), part(m, 0), ss.at[0, m], rs.at[0, m], z1p),
            (m, 2): send(part(m, 1), part(m, 2), ss.at[1, m], rs.at[1, m], z1m),
        }
        for to, mm, j in ((z2p, {0: 3, 3: 2}, 2), (z2m, {0: 0, 1: 1}, 3)):
            if m in mm:
                cps[mm[m], 3] = send(part(m, 1), part(mm[m], 3), ss.at[j, m], rs.at[j, m], to)
        return cps

    def spread_x(a, m, ss, rs):
        return [send(a, a, ss.at[j, m], rs.at[j, m], xs[j]) for j in range(3)]

    near_u, near_d, side_u, side_d = {}, {}, {}, {}

    def first_step(m):
        if m:
            arrive(w_z[m])
            if m == 3:
                w_z[2] = stride(3, 2, 2, z4p)
        near_u.update(spread_near(lambda mm, e: wur.at[mm, e, x], m, wua_ss, wua_rs))
        side_d[m] = spread_x(wdr.at[m, 1, x], m, wdx_ss, wdx_rs)

    def second_step(m):
        arrive([near_u[m, e] for e in (0, 2, 3)])
        side_u[m] = spread_x(wur.at[m, :, x], m, wux_ss, wux_rs)
        arrive(side_d[m])
        near_d.update(spread_near(lambda mm, e: wdr.at[mm, e], m, wda_ss, wda_rs))

    def settle(buf, out):
        for m in range(4):
            for e in range(4):
                at_z = (z + 4 * m + e - 1 + NZ) % NZ
                out[pl.ds(pl.multiple_of(at_z * 64, 64), 64), :] = buf[m, e].reshape(64, out.shape[1])

    first_step(0)
    arrive(c_x)
    lane1 = iota((1, 128), 1)
    here = cx[x]
    at_z_total = jnp.sum(cx[0] + cx[1] + cx[2] + cx[3], axis=1, keepdims=True)
    cz[0, 1] = jnp.broadcast_to(at_z_total, (1, 128))
    c_z = [
        send(cz.at[0, 1], cz.at[3, 1], c_ss.at[3], c_rs.at[3], z4p),
        send(cz.at[0, 1], cz.at[1, 1], c_ss.at[4], c_rs.at[4], z4m),
    ]
    transpose(xn, nt, c, t)
    transpose(xc, ct, c, t)
    first_step(3)
    first_step(1)
    arrive(c_z)
    c_far = send(cz.at[3, 1], cz.at[2, 1], c_ss.at[5], c_rs.at[5], z4p)
    second_step(0)
    far_n = forward(xn, 0, own_n)
    first_step(2)
    c_far.wait_recv()
    c_near = [
        send(cz.at[:, 1], cz.at[:, 0], c_ss.at[6], c_rs.at[6], z1p),
        send(cz.at[:, 1], cz.at[:, 2], c_ss.at[7], c_rs.at[7], z1m),
    ] + [
        send(cz.at[a, 1], cz.at[b, 3], c_ss.at[j], c_rs.at[j], to)
        for j, a, b, to in ((8, 0, 3, z2p), (9, 3, 2, z2p), (10, 0, 0, z2m), (11, 1, 1, z2m))
    ]
    second_step(3)
    second_step(1)
    second_step(2)
    own_n[2].wait_recv()
    transpose(xn, nt, oc, t)
    transpose(xn, nt, c, tm_)
    transpose(xn, nt, c, tp_)

    far_c = forward(xc, 1, own_c)
    own_c[2].wait_recv()
    transpose(xc, ct, oc, t)
    transpose(xc, ct, c, tm_)
    transpose(xc, ct, c, tp_)
    far_n[2].wait_recv()
    far_n[3].wait_recv()
    transpose(xn, nt, oc, tm_)
    transpose(xn, nt, oc, tp_)

    last_n = forward_far(xn, 0, far_n)
    for m in range(4):
        arrive(side_u[m])
    settle(wur, wu)
    for cc, tt in ((c, t), (oc, t), (c, tm_), (c, tp_), (oc, tm_), (oc, tp_), (c, t2_)):
        up(cc, tt)
    transpose(xn, nt, c, t2_)
    last_c = forward_far(xc, 1, far_c)
    for m in range(4):
        arrive([near_d[m, e] for e in (0, 2, 3)])
    settle(wdr, wd)
    far_c[2].wait_recv()
    far_c[3].wait_recv()
    transpose(xc, ct, oc, tm_)
    transpose(xc, ct, oc, tp_)
    transpose(xc, ct, c, t2_)
    for cc, tt in ((c, t), (oc, t), (c, tm_), (c, tp_), (oc, tm_), (oc, tp_), (c, t2_)):
        back(cc, tt)
    last_n[0].wait_recv()
    last_n[1].wait_recv()
    up(oc, t2_)
    transpose(xn, nt, oc, t2_)
    arrive(c_near)
    before = jnp.zeros((1, 128), F32)
    for m in range(4):
        for e in range(4):
            before = before + jnp.where((z + 4 * m + e - 1 + NZ) % NZ < z, cz[m, e], 0.0)
    beside = jnp.zeros((1, 128), F32)
    for xx in range(NX):
        beside = beside + jnp.where(xx < x, cx[xx], 0.0)
    before_a = before[:, 0:1] + jnp.sum(beside, axis=1, keepdims=True)
    slot1 = lane1.astype(F32)
    pos, totals = [], []
    for g in range(2):
        first = jnp.zeros((1, 1), F32)
        parts = []
        for p in range(4):
            n = jnp.sum(jnp.where(lane1 == 4 * g + p, here, 0.0), axis=1, keepdims=True)
            parts.append(jnp.where(slot1 < n, slot1 + first, NONE))
            first = first + n
        pos.append(jnp.concatenate(parts, axis=1))
        totals.append(first)
    in_cps[1].wait()
    owners = oc_in[...].astype(F32)
    owner_first = jnp.sum(jnp.where(lane1 < 2 * k, owners, 0.0), axis=1, keepdims=True)
    owned = [
        jnp.sum(jnp.where(lane1 == 2 * k + g, owners, 0.0), axis=1, keepdims=True)
        for g in range(2)
    ]
    shift = [owner_first - before_a, owner_first + owned[0] - before_a - totals[0]]
    end_ids = iota((MOVE, CAP), 0).astype(F32)
    group_rows = [hh[4 * g : 4 * g + 4].reshape(CAP, CW) for g in range(2)]

    def ends(g, base):
        table = jnp.where(end_ids + base == pos[g], 1.0, 0.0).astype(BF16)
        return dot(table, group_rows[g]).astype(BF16)

    hs[0] = ends(0, 0.0)
    hs[1] = ends(1, totals[1] - MOVE)
    h_p = send(hs.at[0], hr.at[0], h_ss.at[0], h_rs.at[0], k_prev)
    h_n = send(hs.at[1], hr.at[1], h_ss.at[1], h_rs.at[1], k_next)
    first_b = ends(1, 0.0)
    last_a = ends(0, totals[0] - MOVE)

    row_ids = iota((CAP, CAP), 0).astype(F32)
    end_row = iota((CAP, 2 * MOVE), 0).astype(F32)
    end_lane1 = iota((1, 2 * MOVE), 1)
    end_at = end_lane1.astype(F32)

    def place(g, edge):
        inner = jnp.where(
            (row_ids + shift[g] == pos[g]) & (row_ids < owned[g]), 1.0, 0.0
        ).astype(BF16)
        end_pos = jnp.where(end_lane1 < MOVE, end_at - MOVE, end_at - MOVE + totals[g])
        outer = jnp.where(
            (end_row + shift[g] == end_pos) & (end_row < owned[g]), 1.0, 0.0
        ).astype(BF16)
        ho[g] = (dot(inner, group_rows[g]) + dot(outer, edge)).astype(BF16)


    last_c[0].wait_recv()
    last_c[1].wait_recv()
    transpose(xc, ct, oc, t2_)
    back(oc, t2_)

    def grad(m, left_ref, right_ref, g32, gb):
        rows = []
        for e in range(4):
            at_z = (z + 4 * m + e - 1 + NZ) % NZ
            part = pl.ds(pl.multiple_of(at_z * 64, 64), 64)
            rows.append(jnp.concatenate([left_ref[b, part, :] for b in range(8)], axis=1))
        r = dot(jnp.concatenate(rows, axis=0), right_ref[...].reshape(8 * SLOT, CW))
        r = r.reshape(4, NX, 16, CW)
        g32[m] = r
        gb[m] = r.astype(BF16)

    def near_sum(part, m, into, into2, ss, rs):
        to2 = z2p if m < 2 else z2m
        return [
            send(part(m, 2), into.at[0, m], ss.at[0, m], rs.at[0, m], z1p),
            send(part(m, 0), into.at[1, m], ss.at[1, m], rs.at[1, m], z1m),
            send(part(m, 3), into2.at[m], ss.at[2, m], rs.at[2, m], to2),
        ]

    def near_total(own, m, cps, into, into2):
        far = {0: (0, 3), 1: (1,), 2: (), 3: (2,)}[m]
        arrive(cps[m][0:2] + [cps[i][2] for i in far])
        r = own + into[0, m].astype(F32) + into[1, m].astype(F32)
        for i in far:
            r = r + into2[i].astype(F32)
        return r

    def side_total(own, m, cps, into):
        arrive(cps[m])
        return own + into[0, m].astype(F32) + into[1, m].astype(F32) + into[2, m].astype(F32)

    g_dn, g_ux, g_dx, g_un, part_d, part_u = {}, {}, {}, {}, {}, {}

    def start(m):
        grad(m, ct, hh, gd32, gdb)
        g_dn[m] = near_sum(lambda mm, e: gdb.at[mm, e], m, da, da2, gda_ss, gda_rs)
        grad(m, nt, pg, gu32, gub)
        g_ux[m] = [
            send(gub.at[m, :, x_of[j]], ux.at[j, m], gux_ss.at[j, m], gux_rs.at[j, m], xs[j])
            for j in range(3)
        ]

    def d_first(m):
        r = near_total(gd32[m, 1], m, g_dn, da, da2)
        d1[m] = r
        d1b[m] = r.astype(BF16)
        g_dx[m] = [
            send(d1b.at[m, x_of[j]], dx.at[j, m], gdx_ss.at[j, m], gdx_rs.at[j, m], xs[j])
            for j in range(3)
        ]

    def u_first(m):
        r = side_total(gu32[m, :, x], m, g_ux, ux)
        u1[m] = r
        u1b[m] = r.astype(BF16)
        g_un[m] = near_sum(lambda mm, e: u1b.at[mm, e], m, ua, ua2, gua_ss, gua_rs)

    def halves(m):
        return [
            jnp.concatenate([part_u[m][8 * h : 8 * h + 8], part_d[m][8 * h : 8 * h + 8]], axis=0)
            for h in range(2)
        ]

    g_far, g_end = [], {}

    def both_second(m):
        part_d[m] = side_total(d1[m, x], m, g_dx, dx)
        part_u[m] = near_total(u1[m, 1], m, g_un, ua, ua2)
        if m == 2:
            u2b[...] = part_u[m].astype(BF16)
            d2b[...] = part_d[m].astype(BF16)
            g_far.append(send(u2b, ub, gub_ss.at[0], gub_rs.at[0], z4p))
            g_far.append(send(d2b, db, gdb_ss.at[0], gdb_rs.at[0], z4p))
            return
        if m == 1:
            arrive(g_far)
            part_u[m] = part_u[m] + ub[...].astype(F32)
            part_d[m] = part_d[m] + db[...].astype(F32)
        h = halves(m)
        if m == 0:
            s0[0], s0[1] = h
            g_end[m] = [send(s0.at[oc], r0, f_ss, f_rs, sib)]
            return
        slot = {1: 0, 3: 1}[m]
        sb[slot, 0] = h[0].astype(BF16)
        sb[slot, 1] = h[1].astype(BF16)
        same, other = {1: (z4p, z4p_other), 3: (z4m, z4m_other)}[m]
        g_end[m] = [
            send(sb.at[slot, c], rb.at[slot, c], gub_ss.at[m], gub_rs.at[m], same),
            send(sb.at[slot, oc], rb.at[slot, c], gdb_ss.at[m], gdb_rs.at[m], other),
        ]

    def both_first(m):
        d_first(m)
        u_first(m)

    start(2)
    start(1)
    both_first(2)
    start(3)
    both_first(1)
    both_second(2)
    start(0)

    h_p.wait_recv()
    h_n.wait_recv()
    place(0, jnp.concatenate([hr[1], first_b], axis=0))
    place(1, jnp.concatenate([last_a, hr[0]], axis=0))
    h_s = send(ho.at[oc], hq, h_ss.at[2], h_rs.at[2], sib)
    out_own = pltpu.make_async_copy(
        ho.at[c], hid_hbm.at[:, pl.ds(pl.multiple_of(c * CW, CW), CW)], out_sem.at[0]
    )
    out_own.start()

    both_first(3)
    both_second(1)
    both_first(0)
    both_second(3)
    both_second(0)

    h_s.wait_recv()
    out_sib = pltpu.make_async_copy(
        hq, hid_hbm.at[:, pl.ds(pl.multiple_of(oc * CW, CW), CW)], out_sem.at[1]
    )
    out_sib.start()

    arrive(g_end[1] + g_end[3] + g_end[0])
    mine = s0[c] + rb[0, c].astype(F32) + rb[1, c].astype(F32)
    other = r0[...] + rb[0, oc].astype(F32) + rb[1, oc].astype(F32)
    low, high = jnp.where(c == 0, mine, other), jnp.where(c == 0, other, mine)
    for i, out in enumerate((gu_out, gd_out)):
        out[:, 0:CW] = low[8 * i : 8 * i + 8]
        out[:, CW:] = high[8 * i : 8 * i + 8]

    for cp in sends:
        cp.wait_send()
    out_own.wait()
    out_sib.wait()


def body(byte_states, cotangent, w_up, w_down, bounds, owner_counts):
    vmem = pl.BlockSpec(memory_space=pltpu.VMEM)
    hbm = pl.BlockSpec(memory_space=pltpu.HBM)
    dma = pltpu.SemaphoreType.DMA
    parts = (4, 4, NX, 16, CW)
    scratch = [
        pltpu.VMEM((BD, DB), BF16),
        pltpu.VMEM((BD, DB), BF16),
        pltpu.VMEM((8, 128), jnp.int32),
        pltpu.VMEM((1, 128), jnp.int32),
        pltpu.VMEM((2, 16, CW + 128), BF16),
        pltpu.VMEM((16, CW + 128), BF16),
        pltpu.VMEM(parts, BF16),
        pltpu.VMEM(parts, BF16),
        pltpu.VMEM((DB, CW), BF16),
        pltpu.VMEM((DB, CW), BF16),
        pltpu.VMEM((2, NY, KLOC, DB), BF16),
        pltpu.VMEM((2, NY, KLOC, DB), BF16),
        pltpu.VMEM((8, DB, SLOT), BF16),
        pltpu.VMEM((8, DB, SLOT), BF16),
        pltpu.VMEM((8, SLOT, CW), BF16),
        pltpu.VMEM((8, SLOT, CW), BF16),
        pltpu.VMEM((8, SLOT, CW), F32),
        pltpu.VMEM(parts, F32),
        pltpu.VMEM(parts, BF16),
        pltpu.VMEM(parts, F32),
        pltpu.VMEM(parts, BF16),
        pltpu.VMEM((3, 4, 4, 16, CW), BF16),
        pltpu.VMEM((2, 4, 16, CW), BF16),
        pltpu.VMEM((4, 16, CW), BF16),
        pltpu.VMEM((16, CW), BF16),
        pltpu.VMEM((4, 4, 16, CW), F32),
        pltpu.VMEM((4, 4, 16, CW), BF16),
        pltpu.VMEM((16, CW), BF16),
        pltpu.VMEM((3, 4, 16, CW), BF16),
        pltpu.VMEM((2, 4, NX, 16, CW), BF16),
        pltpu.VMEM((4, NX, 16, CW), BF16),
        pltpu.VMEM((16, CW), BF16),
        pltpu.VMEM((4, NX, 16, CW), F32),
        pltpu.VMEM((4, NX, 16, CW), BF16),
        pltpu.VMEM((16, CW), BF16),
        pltpu.VMEM((2, MOVE, CW), BF16),
        pltpu.VMEM((2, MOVE, CW), BF16),
        pltpu.VMEM((2, CAP, CW), BF16),
        pltpu.VMEM((CAP, CW), BF16),
        pltpu.VMEM((NX, 1, 128), F32),
        pltpu.VMEM((4, 4, 1, 128), F32),
        pltpu.VMEM((2, 2, 16, CW), BF16),
        pltpu.VMEM((2, 2, 16, CW), BF16),
        pltpu.VMEM((2, 16, CW), F32),
        pltpu.VMEM((16, CW), F32),
        dma((4,)),
        dma((2,)),
        dma, dma,
        dma((3,)), dma((3,)), dma((4, 4)), dma((4, 4)), dma((3, 4)), dma((3, 4)),
        dma((3,)), dma((3,)), dma((4, 4)), dma((4, 4)), dma((3, 4)), dma((3, 4)),
        dma((2, 4)), dma((2, 4)), dma((2, 5)), dma((2, 5)),
        dma((3, 4)), dma((3, 4)), dma((3, 4)), dma((3, 4)), dma((4,)), dma((4,)),
        dma((3, 4)), dma((3, 4)), dma((3, 4)), dma((3, 4)), dma((4,)), dma((4,)),
        dma((3,)), dma((3,)), dma, dma,
        dma((12,)), dma((12,)),
    ]
    hidden, grad_up, grad_down = pl.pallas_call(
        kernel,
        out_shape=(
            jax.ShapeDtypeStruct((CAP, 2 * CW), BF16),
            jax.ShapeDtypeStruct((8, 2 * CW), F32),
            jax.ShapeDtypeStruct((8, 2 * CW), F32),
        ),
        in_specs=[hbm, hbm, vmem, vmem, hbm, hbm],
        out_specs=(hbm, vmem, vmem),
        scratch_shapes=scratch,
        compiler_params=pltpu.CompilerParams(
            collective_id=0, has_side_effects=True, vmem_limit_bytes=48 * 1024 * 1024
        ),
        cost_estimate=pl.CostEstimate(
            flops=4 * 10**9, bytes_accessed=2 * 1024 * 1024, transcendentals=262144
        ),
    )(
        *(
            pltpu.with_memory_space_constraint(a, pltpu.HBM)
            for a in (
                byte_states,
                cotangent,
                w_up,
                w_down.T,
                bounds.reshape(8, 128),
                owner_counts.reshape(1, 128),
            )
        )
    )
    return hidden, grad_up, grad_down.T


def solution(mesh):
    return jax.shard_map(
        body,
        mesh=mesh,
        in_specs=(
            P(("seq", "tp"), None),
            P(("seq", "tp"), None),
            P("seq", "tp"),
            P("tp", "seq"),
            P("seq"),
            P(),
        ),
        out_specs=(P("seq", "tp"), P("seq", "tp"), P("tp", "seq")),
        check_vma=False,
    )
```

time: 75.2 us -> 62.4 us (0.83)
  Pallas kernels: 68 us -> 59.5 us
  local copies, waits for them, and re-layouts: 6.15 us -> 2.01 us
    pallas_call x1, Pallas kernels: 68 us -> 59.5 us  [body(): pl.pallas_call(kernel, out_shape=(jax.ShapeDtypeStruct((CAP, 2 * CW), BF1...]
    unnamed x15 -> x3, local copies, waits for them, and re-layouts: 6.15 us -> 2.01 us
where the time goes in v2:
time: 62.4 us; the launch traced here: 62.1 us
  Pallas kernels  59.5 us (95%)
  local copies, waits for them, and re-layouts  2.01 us (3%)
  between operations  0.64 us (1%)
    pallas_call x1, Pallas kernels, body(): pl.pallas_call(kernel, out_shape=(jax.ShapeDtypeStruct((CAP, 2 * CW), BF1...  59.5 us
    unnamed x3, local copies, waits for them, and re-layouts  2.01 us

profile of v2, /device:TPU:1, one launch (start us, length us, event | category | flops | bytes accessed | tf_op | source)
XLA Modules:
  0.0 62.1 jit_solution(3820511982954209985)
XLA Ops:
  0.6 59.5 %shard_map.85 = (bf16[512,512]{1,0:T(8,128)(2,1)S(1)}, f32[8,512]{1,0:T(8,128)S(1)}, f32[8,512]{1,0:T(8,128)S(1)}) custom-call(bf16[256,1024]{1,0:T(8,128)(2,1)} %bs_hbm.1, bf16[256,1024]{1,0:T(8,128)(2,1)} %co_hbm.1, bf16[8,512]{1,0:T(8,128)(2,1)} %wu_in.1, bf16[8,512]{1,0:T(8,128)(2,1)} %bitcast.5, s32[8,128]{1,0:T(8,128)} %bitcast.6, s32[1,128]{1,0:T(1,128)} %bitcast.7), custom_call_target="tpu_custom_call" | custom-call | flops 4000000000 | bytes 2097152 | tf_op jit(solution)/shard_map/pallas_call | solution.py:587
  60.1 0.8 %copy.12 = bf16[512,512]{1,0:T(8,128)(2,1)} copy(bf16[512,512]{1,0:T(8,128)(2,1)S(1)} %get-tuple-element.12) | data formatting | bytes 1048576
  60.9 0.6 copy.13
  61.5 0.6 copy.14

commit v3 on v2

--- a/solution.py
+++ b/solution.py
@@ -40,9 +40,9 @@
 
 
 def kernel(
-    bs_hbm, co_hbm, wu_in, wd_in, marks_hbm, oc_hbm,
+    bs_hbm, co_hbm, wu_hbm, wd_hbm, marks_hbm, oc_hbm,
     hid_hbm, gu_out, gd_out,
-    bs, co, marks_in, oc_in, pw, rw, wur, wdr, wu, wd, xn, xc, nt, ct, hh, pg, ff,
+    bs, co, marks_in, oc_in, wu_in, wd_in, pw, rw, wur, wdr, wu, wd, xn, xc, nt, ct, hh, pg, ff,
     gu32, gub, gd32, gdb,
     ux, ua, ua2, ub, u1, u1b, u2b,
     dx, da, da2, db, d1, d1b, d2b,
@@ -95,12 +95,20 @@
     in_cps = [
         pltpu.make_async_copy(a, b, in_sem.at[i])
         for i, (a, b) in enumerate(
-            ((marks_hbm, marks_in), (oc_hbm, oc_in), (bs_hbm, bs), (co_hbm, co))
+            (
+                (marks_hbm, marks_in),
+                (oc_hbm, oc_in),
+                (bs_hbm, bs),
+                (co_hbm, co),
+                (wu_hbm, wu_in),
+                (wd_hbm, wd_in),
+            )
         )
     ]
     for cp in in_cps:
         cp.start()
-    in_cps[0].wait()
+    for i in (0, 4, 5):
+        in_cps[i].wait()
 
     marks = marks_in[...].astype(F32)
     row8 = iota((8, 128), 0)
@@ -187,15 +195,18 @@
                 eye, rows[:, j * 256 : (j + 1) * 256]
             ).astype(BF16)
 
-    def up(cc, tt):
-        v = dot(rows_of(xn, cc, tt), wu[...])
+    hh[:, KLOC:, :] = jnp.zeros((8, SLOT - KLOC, CW), BF16)
+    pg[:, KLOC:, :] = jnp.zeros((8, SLOT - KLOC, CW), BF16)
+
+    def up(cc):
+        v = dot(xn[cc].reshape(NY * KLOC, DB), wu[...])
         sg = jax.nn.sigmoid(v)
-        hh[cc * 4 + tt] = (v * sg).astype(BF16)
-        ff[cc * 4 + tt] = sg * (1.0 + v * (1.0 - sg))
-
-    def back(cc, tt):
-        v = dot(rows_of(xc, cc, tt), wd[...])
-        pg[cc * 4 + tt] = (v * ff[cc * 4 + tt]).astype(BF16)
+        hh[pl.ds(cc * 4, 4), 0:KLOC, :] = (v * sg).astype(BF16).reshape(NY, KLOC, CW)
+        ff[cc] = sg * (1.0 + v * (1.0 - sg))
+
+    def back(cc):
+        v = dot(xc[cc].reshape(NY * KLOC, DB), wd[...])
+        pg[pl.ds(cc * 4, 4), 0:KLOC, :] = (v * ff[cc]).astype(BF16).reshape(NY, KLOC, CW)
 
     def arrive(cps):
         for cp in cps:
@@ -298,27 +309,26 @@
     transpose(xn, nt, oc, tp_)
 
     last_n = forward_far(xn, 0, far_n)
-    for m in range(4):
-        arrive(side_u[m])
-    settle(wur, wu)
-    for cc, tt in ((c, t), (oc, t), (c, tm_), (c, tp_), (oc, tm_), (oc, tp_), (c, t2_)):
-        up(cc, tt)
     transpose(xn, nt, c, t2_)
     last_c = forward_far(xc, 1, far_c)
-    for m in range(4):
-        arrive([near_d[m, e] for e in (0, 2, 3)])
-    settle(wdr, wd)
     far_c[2].wait_recv()
     far_c[3].wait_recv()
     transpose(xc, ct, oc, tm_)
     transpose(xc, ct, oc, tp_)
-    transpose(xc, ct, c, t2_)
-    for cc, tt in ((c, t), (oc, t), (c, tm_), (c, tp_), (oc, tm_), (oc, tp_), (c, t2_)):
-        back(cc, tt)
     last_n[0].wait_recv()
     last_n[1].wait_recv()
-    up(oc, t2_)
     transpose(xn, nt, oc, t2_)
+    for m in range(4):
+        arrive(side_u[m])
+    settle(wur, wu)
+    up(c)
+    up(oc)
+    transpose(xc, ct, c, t2_)
+    for m in range(4):
+        arrive([near_d[m, e] for e in (0, 2, 3)])
+    settle(wdr, wd)
+    back(c)
+
     arrive(c_near)
     before = jnp.zeros((1, 128), F32)
     for m in range(4):
@@ -380,7 +390,7 @@
     last_c[0].wait_recv()
     last_c[1].wait_recv()
     transpose(xc, ct, oc, t2_)
-    back(oc, t2_)
+    back(oc)
 
     def grad(m, left_ref, right_ref, g32, gb):
         rows = []
@@ -482,9 +492,9 @@
     start(1)
     both_first(2)
     start(3)
+    start(0)
     both_first(1)
     both_second(2)
-    start(0)
 
     h_p.wait_recv()
     h_n.wait_recv()
@@ -532,6 +542,8 @@
         pltpu.VMEM((BD, DB), BF16),
         pltpu.VMEM((8, 128), jnp.int32),
         pltpu.VMEM((1, 128), jnp.int32),
+        pltpu.VMEM((8, 2 * CW), BF16),
+        pltpu.VMEM((8, 2 * CW), BF16),
         pltpu.VMEM((2, 16, CW + 128), BF16),
         pltpu.VMEM((16, CW + 128), BF16),
         pltpu.VMEM(parts, BF16),
@@ -544,7 +556,7 @@
         pltpu.VMEM((8, DB, SLOT), BF16),
         pltpu.VMEM((8, SLOT, CW), BF16),
         pltpu.VMEM((8, SLOT, CW), BF16),
-        pltpu.VMEM((8, SLOT, CW), F32),
+        pltpu.VMEM((2, NY * KLOC, CW), F32),
         pltpu.VMEM(parts, F32),
         pltpu.VMEM(parts, BF16),
         pltpu.VMEM(parts, F32),
@@ -573,7 +585,7 @@
         pltpu.VMEM((2, 2, 16, CW), BF16),
         pltpu.VMEM((2, 16, CW), F32),
         pltpu.VMEM((16, CW), F32),
-        dma((4,)),
+        dma((6,)),
         dma((2,)),
         dma, dma,
         dma((3,)), dma((3,)), dma((4, 4)), dma((4, 4)), dma((3, 4)), dma((3, 4)),
@@ -591,7 +603,7 @@
             jax.ShapeDtypeStruct((8, 2 * CW), F32),
             jax.ShapeDtypeStruct((8, 2 * CW), F32),
         ),
-        in_specs=[hbm, hbm, vmem, vmem, hbm, hbm],
+        in_specs=[hbm] * 6,
         out_specs=(hbm, vmem, vmem),
         scratch_shapes=scratch,
         compiler_params=pltpu.CompilerParams(

time: 62.4 us -> 61 us (0.978)
  Pallas kernels: 59.5 us -> 58.3 us
    pallas_call x1, Pallas kernels: 59.5 us -> 58.3 us  [body(): pl.pallas_call(kernel, out_shape=(jax.ShapeDtypeStruct((CAP, 2 * CW), BF1...]
where the time goes in v3:
time: 61 us; the launch traced here: 60.9 us
  Pallas kernels  58.3 us (96%)
  local copies, waits for them, and re-layouts  2.01 us (3%)
  between operations  0.64 us (1%)
    pallas_call x1, Pallas kernels, body(): pl.pallas_call(kernel, out_shape=(jax.ShapeDtypeStruct((CAP, 2 * CW), BF1...  58.3 us
    unnamed x3, local copies, waits for them, and re-layouts  2.01 us

profile of v3, /device:TPU:1, one launch (start us, length us, event | category | flops | bytes accessed | tf_op | source)
XLA Modules:
  0.0 60.9 jit_solution(17085137263569225087)
XLA Ops:
  0.6 58.3 %shard_map.85 = (bf16[512,512]{1,0:T(8,128)(2,1)S(1)}, f32[8,512]{1,0:T(8,128)S(1)}, f32[8,512]{1,0:T(8,128)S(1)}) custom-call(bf16[256,1024]{1,0:T(8,128)(2,1)} %bs_hbm.1, bf16[256,1024]{1,0:T(8,128)(2,1)} %co_hbm.1, bf16[8,512]{1,0:T(8,128)(2,1)} %wu_hbm.1, bf16[8,512]{1,0:T(8,128)(2,1)} %bitcast.5, s32[8,128]{1,0:T(8,128)} %bitcast.6, s32[1,128]{1,0:T(1,128)} %bitcast.7), custom_call_target="tpu_custom_call" | custom-call | flops 4000000000 | bytes 2097152 | tf_op jit(solution)/shard_map/pallas_call | solution.py:599
  58.9 0.8 %copy.12 = bf16[512,512]{1,0:T(8,128)(2,1)} copy(bf16[512,512]{1,0:T(8,128)(2,1)S(1)} %get-tuple-element.12) | data formatting | bytes 1048576
  59.7 0.6 copy.13
  60.3 0.6 copy.14

commit v4 on v3

--- a/solution.py
+++ b/solution.py
@@ -41,7 +41,7 @@
 
 def kernel(
     bs_hbm, co_hbm, wu_hbm, wd_hbm, marks_hbm, oc_hbm,
-    hid_hbm, gu_out, gd_out,
+    hid_hbm, g_out,
     bs, co, marks_in, oc_in, wu_in, wd_in, pw, rw, wur, wdr, wu, wd, xn, xc, nt, ct, hh, pg, ff,
     gu32, gub, gd32, gdb,
     ux, ua, ua2, ub, u1, u1b, u2b,
@@ -291,6 +291,7 @@
         for j, a, b, to in ((8, 0, 3, z2p), (9, 3, 2, z2p), (10, 0, 0, z2m), (11, 1, 1, z2m))
     ]
     second_step(3)
+    far_c = forward(xc, 1, own_c)
     second_step(1)
     second_step(2)
     own_n[2].wait_recv()
@@ -298,7 +299,6 @@
     transpose(xn, nt, c, tm_)
     transpose(xn, nt, c, tp_)
 
-    far_c = forward(xc, 1, own_c)
     own_c[2].wait_recv()
     transpose(xc, ct, oc, t)
     transpose(xc, ct, c, tm_)
@@ -522,9 +522,8 @@
     mine = s0[c] + rb[0, c].astype(F32) + rb[1, c].astype(F32)
     other = r0[...] + rb[0, oc].astype(F32) + rb[1, oc].astype(F32)
     low, high = jnp.where(c == 0, mine, other), jnp.where(c == 0, other, mine)
-    for i, out in enumerate((gu_out, gd_out)):
-        out[:, 0:CW] = low[8 * i : 8 * i + 8]
-        out[:, CW:] = high[8 * i : 8 * i + 8]
+    g_out[:, 0:CW] = low
+    g_out[:, CW:] = high
 
     for cp in sends:
         cp.wait_send()
@@ -596,15 +595,14 @@
         dma((3,)), dma((3,)), dma, dma,
         dma((12,)), dma((12,)),
     ]
-    hidden, grad_up, grad_down = pl.pallas_call(
+    hidden, grads = pl.pallas_call(
         kernel,
         out_shape=(
             jax.ShapeDtypeStruct((CAP, 2 * CW), BF16),
-            jax.ShapeDtypeStruct((8, 2 * CW), F32),
-            jax.ShapeDtypeStruct((8, 2 * CW), F32),
+            jax.ShapeDtypeStruct((16, 2 * CW), F32),
         ),
         in_specs=[hbm] * 6,
-        out_specs=(hbm, vmem, vmem),
+        out_specs=(hbm, vmem),
         scratch_shapes=scratch,
         compiler_params=pltpu.CompilerParams(
             collective_id=0, has_side_effects=True, vmem_limit_bytes=48 * 1024 * 1024
@@ -625,7 +623,7 @@
             )
         )
     )
-    return hidden, grad_up, grad_down.T
+    return hidden, grads[0:8], grads[8:16].T
 
 
 def solution(mesh):

time: 61 us -> 59.2 us (0.970)
  Pallas kernels: 58.3 us -> 57 us
    pallas_call x1, Pallas kernels: 58.3 us -> 57 us  [body(): pl.pallas_call(kernel, out_shape=(jax.ShapeDtypeStruct((CAP, 2 * CW), BF1...]
    unnamed x3 -> x1, local copies, waits for them, and re-layouts: 2.01 us -> 0.79 us
    transpose x0 -> x1, local copies, waits for them, and re-layouts: none -> 0.61 us  [body(): return (hidden, grads[0:8], grads[8:16].T)]
where the time goes in v4:
time: 59.2 us; the launch traced here: 59 us
  Pallas kernels  57 us (96%)
  local copies, waits for them, and re-layouts  1.41 us (2%)
  between operations  0.64 us (1%)
    pallas_call x1, Pallas kernels, body(): pl.pallas_call(kernel, out_shape=(jax.ShapeDtypeStruct((CAP, 2 * CW), BF1...  57 us

profile of v4, /device:TPU:1, one launch (start us, length us, event | category | flops | bytes accessed | tf_op | source)
XLA Modules:
  0.0 59.0 jit_solution(12856215874293088203)
XLA Ops:
  0.6 57.0 %shard_map.85 = (bf16[512,512]{1,0:T(8,128)(2,1)S(1)}, f32[16,512]{1,0:T(8,128)S(1)}) custom-call(bf16[256,1024]{1,0:T(8,128)(2,1)} %bs_hbm.1, bf16[256,1024]{1,0:T(8,128)(2,1)} %co_hbm.1, bf16[8,512]{1,0:T(8,128)(2,1)} %wu_hbm.1, bf16[8,512]{1,0:T(8,128)(2,1)} %bitcast.5, s32[8,128]{1,0:T(8,128)} %bitcast.6, s32[1,128]{1,0:T(1,128)} %bitcast.7), custom_call_target="tpu_custom_call" | custom-call | flops 4000000000 | bytes 2097152 | tf_op jit(solution)/shard_map/pallas_call | solution.py:598
  57.6 0.6 %slice_bitcast_fusion = (f32[512,8]{0,1:T(8,128)}, f32[8,512]{1,0:T(8,128)}) fusion(f32[16,512]{1,0:T(8,128)S(1)} %get-tuple-element.6), kind=kLoop, calls=%fused_computation | loop fusion | bytes 65536 | tf_op jit(solution)/shard_map/transpose | solution.py:626
  58.2 0.8 %copy.10 = bf16[512,512]{1,0:T(8,128)(2,1)} copy(bf16[512,512]{1,0:T(8,128)(2,1)S(1)} %get-tuple-element.12) | data formatting | bytes 1048576
